TPU v7x, 256 devices: a whole 4x4x8 slice. The times are simulated.
256 devices in a mesh: dp: 32 (over y, x, core), mp: 8 (over z).
Axes of the slice: x: 4, y: 4, z: 8, core: 2. Of those that a mesh axis runs over, the one named last changes fastest.
Arguments:
- patches: bfloat16 [4096, 588], P('dp'), may hold values from -6 to 6
- embed_weight: bfloat16 [6144, 588], P(('mp', 'dp')), may hold values from -0.25 to 0.25
- project_weight: bfloat16 [6144, 3, 3072], P('dp', None, 'mp'), may hold values from -0.078125 to 0.078125
- patch_counts: int32 [256], P('dp'), may hold values from 0 to 64, as said below
- segment_ids: int32 [4096], P('dp'), may hold values from -1 to 255, as said below
- targets: bfloat16 [4096, 3072], P('dp', 'mp'), may hold values from -4 to 4
Outputs:
- project_grad: float32 [6144, 3, 3072], P('dp', None, 'mp')
- loss_value: float32 [], replicated
Inputs may be any that keep to these rules, and one draw needn't show every extreme that they name: `patch_counts`: entry 8 * i + j is the number of patches of image slot j of device i along dp, a multiple of 16, 0 for an empty slot; the counts of one device add up to at most 128, and some device reaches it. `segment_ids`: the rows of device i along dp hold its images whole, slot after slot, each row carrying the id 8 * i + slot of its image, then -1 on the rows left. A device in the upper half of dp holds more rows than the device half the axis away. On each device the images that end after its row 96 cover at most 64 rows. Those rows plus all the rows of the device half the axis away come to at most 96. Both bounds are reached.
All inputs are finite; a program needn't handle non-finite values.
Results may differ from a plain program's by a relative error of at most 0.012.
The roundings to bfloat16 on the way count: a program that leaves them out, or rounds other values in their place, can miss the bound.
Values may be sent and summed in bfloat16 or wider, within the bound.
No kernel may reach another device: no remote copies, remote signals or barrier semaphores. Data moves between devices by JAX's collectives and lax.ppermute only.
A program may use at most 64 MiB of HBM per device.

v0:
```python
import functools
import math

import jax
import jax.numpy as jnp
from jax import lax
from jax.experimental import pallas as pl
from jax.experimental.pallas import tpu as pltpu
from jax.sharding import Mesh
from jax.sharding import PartitionSpec as P

HD = 128
KEEP = 96
MOVE = 64
P_SIZE = 588
PAD_P = 640
SHARE = 16
SHARES = KEEP // SHARE
STATS = 16
SEGMENT = 600
SIDE = 4
CHIPS = 16
CORES = 2
N_MP = 8
DP = ("y", "x", "core")
F32 = jnp.float32
BF16 = jnp.bfloat16
VMEM = pl.BlockSpec(memory_space=pltpu.VMEM)
SMEM = pl.BlockSpec(memory_space=pltpu.SMEM)
ROOM = pltpu.CompilerParams(vmem_limit_bytes=48 * 1024 * 1024)


def shift(array, axis, size, step):
    return lax.ppermute(array, axis, [(i, (i + step) % size) for i in range(size)])


def swap(array):
    return lax.ppermute(array, "core", [(0, 1), (1, 0)])


def turn(array, first, step):
    pairs = []
    for y in range(SIDE):
        for x in range(SIDE):
            for core in range(CORES):
                along_x = (core == 0) == first
                to_y = y if along_x else (y + step) % SIDE
                to_x = (x + step) % SIDE if along_x else x
                pairs.append(((y * SIDE + x) * CORES + core, (to_y * SIDE + to_x) * CORES + core))
    return lax.ppermute(array, DP, pairs)


def rows_kept(counts_ref):
    end = jnp.int32(0)
    kept = jnp.int32(0)
    for slot in range(counts_ref.shape[0]):
        end = end + counts_ref[slot]
        kept = jnp.where(end <= KEEP, end, kept)
    return pl.multiple_of(kept, 16), end


def pack_kernel(counts_ref, *refs):
    sources, (all_ref, leave_ref, wide_ref, tall), rest = refs[:4], refs[4:8], refs[8:]
    places, sem = rest[:4], rest[4]
    copies = [
        pltpu.make_async_copy(source, place, sem.at[index])
        for index, (source, place) in enumerate(zip(sources, places))
    ]
    for copy in copies:
        copy.start()
    for copy in copies:
        copy.wait()
    patch_ref, target_ref, segment_ref, embed_ref = places
    p_size, rows = patch_ref.shape
    tall[...] = jnp.zeros_like(tall)
    tall[:p_size, :] = patch_ref[...].astype(F32)
    marks = jnp.broadcast_to(segment_ref[...].astype(F32) + 1.0, (8, rows))
    tall[SEGMENT : SEGMENT + 8, :] = marks
    all_ref[:rows, :PAD_P] = tall[...].T.astype(BF16)
    all_ref[:rows, PAD_P:] = target_ref[...]
    all_ref[rows:, :] = jnp.zeros((all_ref.shape[0] - rows, all_ref.shape[1]), BF16)
    kept, total = rows_kept(counts_ref)
    leave_ref[...] = all_ref[pl.ds(kept, MOVE), :]
    row = lax.broadcasted_iota(jnp.int32, (wide_ref.shape[0], wide_ref.shape[1] - 512), 0)
    column = lax.broadcasted_iota(jnp.int32, (wide_ref.shape[0], wide_ref.shape[1] - 512), 1)
    here = (row == 0) & (column == p_size - 512)
    wide_ref[:, 512:] = jnp.where(here, total.astype(F32), 0.0).astype(BF16)
    wide_ref[:, :p_size] = embed_ref[...]


def pack(patches, targets, segment_ids, patch_counts, embed_weight):
    rows, p_size = patches.shape
    width = PAD_P + targets.shape[1]
    return pl.pallas_call(
        pack_kernel,
        out_shape=(
            jax.ShapeDtypeStruct((rows + MOVE, width), BF16),
            jax.ShapeDtypeStruct((MOVE, width), BF16),
            jax.ShapeDtypeStruct((embed_weight.shape[0], PAD_P), BF16),
        ),
        in_specs=[SMEM] + [pl.BlockSpec(memory_space=pltpu.HBM)] * 4,
        out_specs=(VMEM, VMEM, VMEM),
        scratch_shapes=[
            pltpu.VMEM((PAD_P, rows), F32),
            pltpu.VMEM((p_size, rows), BF16),
            pltpu.VMEM(targets.shape, BF16),
            pltpu.VMEM((1, rows), jnp.int32),
            pltpu.VMEM(embed_weight.shape, BF16),
            pltpu.SemaphoreType.DMA((4,)),
        ],
        cost_estimate=pl.CostEstimate(flops=1_000_000, bytes_accessed=1_000_000, transcendentals=0),
    )(patch_counts, patches.T, targets, segment_ids.reshape(1, rows), embed_weight)


def embed_kernel(counts_ref, all_ref, come_ref, wide_ref, out_ref, target_ref, column_ref, row_ref, total_ref, around):
    kept, _ = rows_kept(counts_ref)
    around[...] = jnp.zeros_like(around)
    around[pl.ds(kept, MOVE), :] = come_ref[...]
    mine = lax.broadcasted_iota(jnp.int32, (KEEP, 1), 0) < kept
    merged = jnp.where(mine, all_ref[:KEEP, :], around[:KEEP, :])
    target_ref[...] = merged[:, PAD_P:]
    marks = merged[:, PAD_P - 128 : PAD_P].astype(F32)
    slot = lax.broadcasted_iota(jnp.int32, marks.shape, 1) == SEGMENT - (PAD_P - 128)
    mark = jnp.sum(jnp.where(slot, marks, 0.0), axis=1, keepdims=True) - 1.0
    spread = jnp.broadcast_to(mark, marks.shape)
    column_ref[...] = spread.astype(jnp.int32)
    row_ref[...] = spread.T[:8, :].astype(jnp.int32)
    tail = wide_ref[:, PAD_P - 128 : PAD_P].astype(F32)
    slot = lax.broadcasted_iota(jnp.int32, tail.shape, 1) == P_SIZE - (PAD_P - 128)
    total_ref[...] = jnp.full(total_ref.shape, jnp.sum(jnp.where(slot, tail, 0.0)), F32)
    out_ref[...] = dot_t(merged[:, :PAD_P], wide_ref[...]).astype(BF16)


def embed(patch_counts, packed, coming, wide):
    targets = packed.shape[1] - PAD_P
    return pl.pallas_call(
        embed_kernel,
        out_shape=(
            jax.ShapeDtypeStruct((KEEP, wide.shape[0]), BF16),
            jax.ShapeDtypeStruct((KEEP, targets), BF16),
            jax.ShapeDtypeStruct((KEEP, 128), jnp.int32),
            jax.ShapeDtypeStruct((8, KEEP), jnp.int32),
            jax.ShapeDtypeStruct((8, 128), F32),
        ),
        in_specs=[SMEM] + [VMEM] * 3,
        out_specs=(VMEM,) * 5,
        scratch_shapes=[pltpu.VMEM((KEEP + MOVE, packed.shape[1]), BF16)],
        compiler_params=ROOM,
        cost_estimate=pl.CostEstimate(
            flops=100_000_000, bytes_accessed=2_000_000, transcendentals=0
        ),
    )(patch_counts, packed, coming, wide)


def by_parity(values):
    part = [values[:, 128 * i : 128 * (i + 1)] for i in range(6)]
    turned = [pltpu.roll(p, 64, 1) for p in part]
    low = lax.broadcasted_iota(jnp.int32, part[0].shape, 1) < 64
    even = [part[0], jnp.where(low, part[1], turned[3]), jnp.where(low, turned[3], turned[4])]
    odd = [jnp.where(low, turned[1], turned[2]), jnp.where(low, turned[2], part[4]), part[5]]
    return jnp.concatenate(even, axis=1), jnp.concatenate(odd, axis=1)


def norm_kernel(place_ref, *refs):
    blocks, (share_ref, own_ref, other_ref, chips_ref) = refs[:-4], refs[-4:]
    me, core = place_ref[0], place_ref[1]
    width = blocks[0].shape[1]
    values = [b[...].astype(F32) for b in blocks[:-2]]
    values.append(jnp.concatenate([blocks[-2][...], blocks[-1][...]], axis=0).astype(F32))
    offsets = [0]
    for step in range(1, N_MP // 2):
        offsets += [-step, step]
    offsets.append(N_MP // 2)
    features = width * N_MP
    mean = sum(jnp.sum(v, axis=1, keepdims=True) for v in values) / features
    spread = sum(jnp.sum((v - mean) * (v - mean), axis=1, keepdims=True) for v in values)
    scale = lax.rsqrt(spread / features + 1e-06)
    half = width // 2
    for offset, v in zip(offsets, values):
        place = lax.rem(me + offset + N_MP, N_MP)
        normed = (v - mean) * scale
        chips_ref[2 * place] = normed[:, :half].astype(BF16)
        chips_ref[2 * place + 1] = normed[:, half:].astype(BF16)
        even, odd = by_parity(normed)
        first = core == 0
        columns = pl.ds(pl.multiple_of(place * half, 128), half)
        own_ref[:, columns] = jnp.where(first, even, odd).astype(BF16)
        other_ref[:, columns] = jnp.where(first, odd, even).astype(BF16)
    start = pl.multiple_of(jnp.minimum(me, SHARES - 1) * SHARE, SHARE)
    share_ref[...] = chips_ref[:, pl.ds(start, SHARE), :]


def gather_norm(own, place):
    blocks = [own]
    ahead = back = own
    for _ in range(1, N_MP // 2):
        ahead = shift(ahead, "mp", N_MP, 1)
        back = shift(back, "mp", N_MP, -1)
        blocks += [ahead, back]
    half = own.shape[0] // 2
    blocks.append(shift(ahead[:half], "mp", N_MP, 1))
    blocks.append(shift(back[half:], "mp", N_MP, -1))
    rows, width = own.shape
    return pl.pallas_call(
        norm_kernel,
        out_shape=(
            jax.ShapeDtypeStruct((2 * N_MP, SHARE, width // 2), BF16),
            jax.ShapeDtypeStruct((rows, width * N_MP // 2), BF16),
            jax.ShapeDtypeStruct((rows, width * N_MP // 2), BF16),
        ),
        in_specs=[SMEM] + [VMEM] * len(blocks),
        out_specs=(VMEM, VMEM, VMEM),
        scratch_shapes=[pltpu.VMEM((2 * N_MP, rows, width // 2), BF16)],
        compiler_params=ROOM,
        cost_estimate=pl.CostEstimate(flops=4_000_000, bytes_accessed=4_000_000, transcendentals=0),
    )(place, *blocks)


def project_kernel(own_ref, other_ref, weight_ref, own_out, other_out):
    @pl.when(pl.program_id(0) == 0)
    def _():
        own_out[...] = jnp.zeros_like(own_out)
        other_out[...] = jnp.zeros_like(other_out)

    rows = own_ref.shape[0]
    chips, groups = weight_ref.shape[:2]
    left = jnp.concatenate([own_ref[...], other_ref[...]], axis=0)
    right = jnp.concatenate(
        [
            jnp.concatenate([weight_ref[i, group] for group in range(groups)], axis=1)
            for i in range(chips)
        ],
        axis=0,
    )
    product = jnp.dot(left, right, preferred_element_type=F32)
    own_out[...] += product[:rows]
    other_out[...] += product[rows:]


def project(own, other, weight):
    rows = own.shape[0]
    chips, groups, depth, span = weight.shape
    step = 4
    block = pl.BlockSpec((rows, step * depth), lambda i: (0, i))
    result = pl.BlockSpec((rows, groups * span), lambda i: (0, 0))
    return pl.pallas_call(
        project_kernel,
        grid=(chips // step,),
        out_shape=(jax.ShapeDtypeStruct((rows, groups * span), F32),) * 2,
        in_specs=[
            block,
            block,
            pl.BlockSpec((step, groups, depth, span), lambda i: (i, 0, 0, 0)),
        ],
        out_specs=(result, result),
        compiler_params=ROOM,
        cost_estimate=pl.CostEstimate(
            flops=1_360_000_000, bytes_accessed=9_000_000, transcendentals=0
        ),
    )(own, other, weight)


def dot_t(a, b):
    return lax.dot_general(a, b, (((1,), (1,)), ((), ())), preferred_element_type=F32)


def t_dot(a, b):
    return lax.dot_general(a, b, (((0,), (0,)), ((), ())), preferred_element_type=F32)


def norm_parts(values):
    center = values - jnp.mean(values, axis=-1, keepdims=True)
    scale = lax.rsqrt(jnp.mean(center * center, axis=-1, keepdims=True) + 1e-06)
    return center * scale, scale


def norm_grad(normed, scale, cotangent):
    along = jnp.mean(cotangent * normed, axis=-1, keepdims=True)
    return scale * (cotangent - jnp.mean(cotangent, axis=-1, keepdims=True) - normed * along)


def attend_kernel(raw_ref, more_ref, row_ref, column_ref, target_ref, total_ref, grad_ref):
    inverse_root = 1.0 / math.sqrt(HD)
    heads = target_ref.shape[1] // HD
    rows = raw_ref.shape[0]
    row_segment = row_ref[:, :1]
    valid = row_segment >= 0
    allowed = (row_segment == column_ref[:1, :]) & valid
    total = total_ref[:1, :1]
    squares = jnp.zeros((raw_ref.shape[0], HD), F32)
    for head in range(heads):
        cut = [slice((part * heads + head) * HD, (part * heads + head + 1) * HD) for part in range(3)]
        query, key, value = [raw_ref[:, c] + more_ref[:, c] for c in cut]
        query_exact, query_scale = norm_parts(query)
        key_exact, key_scale = norm_parts(key)
        query_normed = query_exact.astype(BF16)
        key_normed = key_exact.astype(BF16)
        value_rows = value.astype(BF16)
        scores = dot_t(query_normed, key_normed) * inverse_root
        exponent = jnp.where(allowed, jnp.exp(scores), 0.0)
        denominator = jnp.sum(exponent, axis=-1, keepdims=True)
        denominator = jnp.where(valid, denominator, 1.0)
        weights = (exponent / denominator).astype(BF16)
        attended = jnp.dot(weights, value_rows, preferred_element_type=F32)
        target = target_ref[:, head * HD : (head + 1) * HD].astype(F32)
        error = jnp.where(valid, attended - target, 0.0)
        squares += error * error
        out_grad = (error / total).astype(BF16)
        prob_grad = dot_t(out_grad, value_rows)
        grad_ref[:rows, cut[2]] = t_dot(weights, out_grad).astype(BF16)
        weight_float = weights.astype(F32)
        inner = jnp.sum(prob_grad * weight_float, axis=-1, keepdims=True)
        score_grad = (weight_float * (prob_grad - inner) * inverse_root).astype(BF16)
        query_cotangent = jnp.dot(score_grad, key_normed, preferred_element_type=F32)
        key_cotangent = t_dot(score_grad, query_normed)
        grad_ref[:rows, cut[0]] = norm_grad(query_exact, query_scale, query_cotangent).astype(BF16)
        grad_ref[:rows, cut[1]] = norm_grad(key_exact, key_scale, key_cotangent).astype(BF16)
    square = jnp.full((STATS, grad_ref.shape[1]), jnp.sum(squares), F32)
    high = square.astype(BF16).astype(F32)
    middle = (square - high).astype(BF16).astype(F32)
    low = square - high - middle
    place = lax.broadcasted_iota(jnp.int32, square.shape, 0)
    terms = jnp.where(place == 0, high, jnp.where(place == 1, middle, low))
    grad_ref[rows:, :] = jnp.where(place < 3, terms, 0.0).astype(BF16)


def attend(raw, more, column, row, targets, patch_total):
    rows, width = raw.shape
    return pl.pallas_call(
        attend_kernel,
        out_shape=jax.ShapeDtypeStruct((rows + STATS, width), BF16),
        in_specs=[VMEM] * 6,
        out_specs=VMEM,
        compiler_params=ROOM,
        cost_estimate=pl.CostEstimate(
            flops=50_000_000, bytes_accessed=1_500_000, transcendentals=30_000
        ),
    )(raw, more, column, row, targets, patch_total)


def turn_kernel(place_ref, blocks_ref, own_ref, other_ref):
    y, x, core = place_ref[0], place_ref[1], place_ref[2]
    half = blocks_ref.shape[3] // 2
    rows = SHARES * SHARE
    ring = (0, -1, 1, 2)
    pieces = []
    for far in ring:
        for near in ring:
            step_x = jnp.where(core == 0, near, far)
            step_y = jnp.where(core == 0, far, near)
            chip = lax.rem(y + step_y + SIDE, SIDE) * SIDE + lax.rem(x + step_x + SIDE, SIDE)
            pieces += [blocks_ref[share, chip] for share in range(SHARES)]
    for group in range(SIDE):
        several = pieces[group * SIDE * SHARES : (group + 1) * SIDE * SHARES]
        wide = jnp.concatenate(several, axis=0).astype(F32).T.astype(BF16)
        columns = slice(group * SIDE * rows, (group + 1) * SIDE * rows)
        first = core == 0
        own_ref[:, columns] = jnp.where(first, wide[:half], wide[half:])
        other_ref[:, columns] = jnp.where(first, wide[half:], wide[:half])


def turn_blocks(blocks, place):
    _, chips, _, feats = blocks.shape
    return pl.pallas_call(
        turn_kernel,
        out_shape=(jax.ShapeDtypeStruct((feats // 2, chips * KEEP), BF16),) * 2,
        in_specs=[SMEM, VMEM],
        out_specs=(VMEM, VMEM),
        compiler_params=ROOM,
        cost_estimate=pl.CostEstimate(flops=1_000_000, bytes_accessed=2_400_000, transcendentals=0),
    )(place, blocks)


def grad_kernel(parts, own_ref, other_ref, *refs):
    pieces, (own_out, other_out) = refs[:parts], refs[parts:]
    for left_ref, out_ref in ((other_ref, other_out), (own_ref, own_out)):
        groups, _, span = out_ref.shape
        total = None
        start = 0
        for piece in pieces:
            rows = piece.shape[0]
            product = jnp.dot(
                left_ref[:, start : start + rows], piece[...], preferred_element_type=F32
            )
            total = product if total is None else total + product
            start += rows
        for group in range(groups):
            out_ref[group] = total[:, group * span : (group + 1) * span]


def grad_first(own, other, pieces, groups):
    width = pieces[0].shape[1]
    part = jax.ShapeDtypeStruct((groups, own.shape[0], width // groups), F32)
    return pl.pallas_call(
        functools.partial(grad_kernel, len(pieces)),
        out_shape=(part, part),
        in_specs=[VMEM] * (2 + len(pieces)),
        out_specs=(VMEM, VMEM),
        compiler_params=ROOM,
        cost_estimate=pl.CostEstimate(
            flops=1_000_000_000, bytes_accessed=5_000_000, transcendentals=0
        ),
    )(own, other, *pieces)


def last_kernel(start, left_ref, piece_ref, part_ref, out_ref):
    rows = piece_ref.shape[0]
    product = jnp.dot(
        left_ref[:, start : start + rows], piece_ref[...], preferred_element_type=F32
    )
    groups, _, span = out_ref.shape
    for group in range(groups):
        out_ref[group] = part_ref[group] + product[:, group * span : (group + 1) * span]


def grad_last(left, piece, part):
    return pl.pallas_call(
        functools.partial(last_kernel, left.shape[1] - piece.shape[0]),
        out_shape=jax.ShapeDtypeStruct(part.shape, F32),
        in_specs=[VMEM] * 3,
        out_specs=VMEM,
        compiler_params=ROOM,
        cost_estimate=pl.CostEstimate(
            flops=170_000_000, bytes_accessed=3_000_000, transcendentals=0
        ),
    )(left, piece, part)


def finish_kernel(a_ref, b_ref, sum_ref, more_ref, total_ref, out_ref, loss_ref):
    out_ref[...] = a_ref[...] + b_ref[...]
    squared = sum_ref[:1, :1] + more_ref[:1, :1]
    loss_ref[...] = squared / (2.0 * total_ref[:1, :1])


def finish(a, b, squared, more, total):
    return pl.pallas_call(
        finish_kernel,
        out_shape=(jax.ShapeDtypeStruct(a.shape, F32), jax.ShapeDtypeStruct((1, 1), F32)),
        in_specs=[VMEM] * 5,
        out_specs=(VMEM, VMEM),
        compiler_params=ROOM,
        cost_estimate=pl.CostEstimate(flops=300_000, bytes_accessed=2_700_000, transcendentals=0),
    )(a, b, squared, more, total)


def near_kernel(*refs):
    blocks, (out_ref, sum_ref) = refs[:-2], refs[-2:]
    rows = blocks[0].shape[0] - STATS
    terms = 0.0
    for index, block in enumerate(blocks):
        out_ref[index * rows : (index + 1) * rows, :] = block[:rows, :]
        terms += block[rows:, :128].astype(F32)
    sum_ref[...] = jnp.broadcast_to(jnp.sum(terms, axis=0, keepdims=True), sum_ref.shape)


def near_rows(blocks):
    rows, width = blocks[0].shape
    return pl.pallas_call(
        near_kernel,
        out_shape=(
            jax.ShapeDtypeStruct((len(blocks) * (rows - STATS), width), BF16),
            jax.ShapeDtypeStruct((8, 128), F32),
        ),
        in_specs=[VMEM] * len(blocks),
        out_specs=(VMEM, VMEM),
        compiler_params=ROOM,
        cost_estimate=pl.CostEstimate(flops=100_000, bytes_accessed=1_800_000, transcendentals=0),
    )(*blocks)


def local(patches, embed_weight, project_weight, patch_counts, segment_ids, targets):
    whole_weight = lax.all_gather(project_weight.transpose(1, 0, 2), ("y", "x"), axis=0)
    y, x, core, mp = [lax.axis_index(a) for a in ("y", "x", "core", "mp")]

    packed, leaving, embed_part = pack(patches, targets, segment_ids, patch_counts, embed_weight)
    half = CHIPS * CORES // 2
    coming = lax.ppermute(leaving, DP, [(i + half, i) for i in range(half)])
    wide = lax.all_gather(embed_part, DP, axis=0, tiled=True)
    own_features, targets, column, row, total_tile = embed(patch_counts, packed, coming, wide)
    chip_blocks, own_half, other_half = gather_norm(own_features, jnp.stack([mp, core]))
    chip_share = lax.all_to_all(chip_blocks, ("y", "x"), split_axis=0, concat_axis=0, tiled=True)
    more_half, chip_share = lax.optimization_barrier((swap(other_half), chip_share))
    chip_rows = lax.all_gather(chip_share, "mp", axis=0)
    own_part, other_part = project(own_half, more_half, whole_weight)
    grad_rows = attend(own_part, swap(other_part), column, row, targets, total_tile)

    near, tile = near_rows(
        lax.optimization_barrier(
            (
                grad_rows,
                turn(grad_rows, True, 1),
                turn(grad_rows, True, -1),
                turn(grad_rows, True, 2),
            )
        )
    )
    behind, ahead = turn(near, False, 1), turn(near, False, -1)
    tile = sum((shift(tile, "mp", N_MP, step) for step in (1, 2, 3)), tile)
    tile = tile + turn(tile, False, -1)
    behind, ahead, tile = lax.optimization_barrier((behind, ahead, tile))
    opposite = turn(behind, False, 1)
    tile = tile + shift(tile, "mp", N_MP, 4)
    tile = tile + turn(tile, False, -2)
    own_left, other_left = turn_blocks(chip_rows, jnp.stack([y, x, core]))
    groups = project_weight.shape[1]
    own_grad, other_grad = grad_first(own_left, other_left, (near, behind, ahead), groups)
    opposite, tile, own_grad, other_grad = lax.optimization_barrier(
        (opposite, tile, own_grad, other_grad)
    )
    more_grad, more_tile = lax.optimization_barrier(
        (swap(grad_last(other_left, opposite, other_grad)), swap(tile))
    )
    weight_grad, loss_tile = finish(
        grad_last(own_left, opposite, own_grad), more_grad, tile, more_tile, total_tile
    )
    loss_value = loss_tile[0, 0]
    return (weight_grad.transpose(1, 0, 2), loss_value)


def solution(mesh):
    chips = Mesh(mesh.devices.reshape(SIDE, SIDE, CORES, N_MP), DP + ("mp",))
    in_specs = (
        P(DP, None),
        P(("mp",) + DP, None),
        P(DP, None, "mp"),
        P(DP),
        P(DP),
        P(DP, "mp"),
    )
    out_specs = (P(DP, None, "mp"), P())
    return jax.shard_map(
        local, mesh=chips, in_specs=in_specs, out_specs=out_specs, check_vma=False
    )
```

profile of v0, /device:TPU:1, one launch (start us, length us, event | category | flops | bytes accessed | tf_op | source)
XLA Modules:
  0.0 153.0 jit_solution(832912677105897048)
XLA Ops:
  7.9 2.6 %shard_map.77 = (bf16[192,1024]{1,0:T(8,128)(2,1)}, bf16[64,1024]{1,0:T(8,128)(2,1)}, bf16[24,640]{1,0:T(8,128)(2,1)}) custom-call(s32[8]{0:T(128)} %counts_ref.3, bf16[588,128]{1,0:T(8,128)(2,1)} %bitcast.14, bf16[128,384]{1,0:T(8,128)(2,1)} %refs_1_.1, s32[1,128]{1,0:T(1,128)} %bitcast.15, bf16[24,588]{1,0:T(8,128)(2,1)} %refs_3_.1), custom_call_target="tpu_custom_call" | custom-call | flops 1000000 | bytes 1000000 | tf_op jit(solution)/shard_map/pallas_call | solution.py:94
  11.8 29.1 %all_gather.15.wide_ref = bf16[768,640]{1,0:T(8,128)(2,1)S(1)} all-gather(bf16[24,640]{1,0:T(8,128)(2,1)} %get-tuple-element.40), channel_id=1, replica_groups=mesh['y'=4,'x'=4,'core'=2,'mp'=8] {'y','x','core'}, dimensions={0}, use_global_device_ids=true | all-gather | bytes 1013760 | tf_op jit(solution)/shard_map/all_gather | solution.py:478
  45.3 4.2 %collective-permute-start.2 = (bf16[96,768]{1,0:T(8,128)(2,1)S(1)}, bf16[96,768]{1,0:T(8,128)(2,1)S(1)}, u32[]{:S(2)}, u32[]{:S(2)}) collective-permute-start(bf16[96,768]{1,0:T(8,128)(2,1)S(1)} %get-tuple-element.41.refs_0_), channel_id=1, source_target_pairs={{0,7},{1,0},{2,1},{3,2},{4,3},{5,4},{6,5},{7,6},{8,15},{9,8},{10,9... | collective-permute-start | bytes 442376 | tf_op jit(solution)/shard_map/ppermute | solution.py:34
  49.5 4.0 %collective-permute-done.1.refs_1_ = bf16[96,768]{1,0:T(8,128)(2,1)S(1)} collective-permute-done((bf16[96,768]{1,0:T(8,128)(2,1)S(1)}, bf16[96,768]{1,0:T(8,128)(2,1)S(1)}, u32[]{:S(2)}, u32[]{:S(2)}) %collective-permute-start.1) | collective-permute-done | bytes 147488 | tf_op jit(solution)/shard_map/ppermute | solution.py:34
  53.5 2.7 %collective-permute-start.4 = (bf16[96,768]{1,0:T(8,128)(2,1)S(1)}, bf16[96,768]{1,0:T(8,128)(2,1)S(1)}, u32[]{:S(2)}, u32[]{:S(2)}) collective-permute-start(bf16[96,768]{1,0:T(8,128)(2,1)S(1)} %collective-permute-done.2.refs_2_), channel_id=1, source_target_pairs={{0,7},{1,0},{2,1},{3,2},{4,3},{5,4},{6,5},{7,6},{8,15},{9,8},{10,9... | collective-permute-start | bytes 442376 | tf_op jit(solution)/shard_map/ppermute | solution.py:34
  56.2 3.3 %collective-permute-done.3.refs_3_ = bf16[96,768]{1,0:T(8,128)(2,1)S(1)} collective-permute-done((bf16[96,768]{1,0:T(8,128)(2,1)S(1)}, bf16[96,768]{1,0:T(8,128)(2,1)S(1)}, u32[]{:S(2)}, u32[]{:S(2)}) %collective-permute-start.3) | collective-permute-done | bytes 147488 | tf_op jit(solution)/shard_map/ppermute | solution.py:34
  59.5 2.7 %collective-permute-start.6 = (bf16[96,768]{1,0:T(8,128)(2,1)S(1)}, bf16[96,768]{1,0:T(8,128)(2,1)S(1)}, u32[]{:S(2)}, u32[]{:S(2)}) collective-permute-start(bf16[96,768]{1,0:T(8,128)(2,1)S(1)} %collective-permute-done.4.refs_4_), channel_id=1, source_target_pairs={{0,7},{1,0},{2,1},{3,2},{4,3},{5,4},{6,5},{7,6},{8,15},{9,8},{10,9... | collective-permute-start | bytes 442376 | tf_op jit(solution)/shard_map/ppermute | solution.py:34
  62.1 2.9 %collective-permute-done.5.refs_5_ = bf16[96,768]{1,0:T(8,128)(2,1)S(1)} collective-permute-done((bf16[96,768]{1,0:T(8,128)(2,1)S(1)}, bf16[96,768]{1,0:T(8,128)(2,1)S(1)}, u32[]{:S(2)}, u32[]{:S(2)}) %collective-permute-start.5) | collective-permute-done | bytes 147488 | tf_op jit(solution)/shard_map/ppermute | solution.py:34
  65.1 2.7 %collective-permute-start.8 = (bf16[48,768]{1,0:T(8,128)(2,1)S(1)}, bf16[48,768]{1,0:T(8,128)(2,1)S(1)}, u32[]{:S(2)}, u32[]{:S(2)}) collective-permute-start(bf16[48,768]{1,0:T(8,128)(2,1)S(1)} %slice.9), channel_id=1, source_target_pairs={{0,7},{1,0},{2,1},{3,2},{4,3},{5,4},{6,5},{7,6},{8,15},{9,8},{10,9... | collective-permute-start | bytes 221192 | tf_op jit(solution)/shard_map/ppermute | solution.py:34
  67.9 2.0 %collective-permute-done.7.refs_7_ = bf16[48,768]{1,0:T(8,128)(2,1)S(1)} collective-permute-done((bf16[48,768]{1,0:T(8,128)(2,1)S(1)}, bf16[48,768]{1,0:T(8,128)(2,1)S(1)}, u32[]{:S(2)}, u32[]{:S(2)}) %collective-permute-start.7) | collective-permute-done | bytes 73760 | tf_op jit(solution)/shard_map/ppermute | solution.py:34
  71.7 3.1 %collective-permute-start.9 = (bf16[96,3072]{1,0:T(8,128)(2,1)S(1)}, bf16[96,3072]{1,0:T(8,128)(2,1)S(1)}, u32[]{:S(2)}, u32[]{:S(2)}) collective-permute-start(bf16[96,3072]{1,0:T(8,128)(2,1)S(1)} %get-tuple-element.42), channel_id=1, source_target_pairs={{0,8},{8,0},{1,9},{9,1},{2,10},{10,2},{3,11},{11,3},{4,12},{12,4},... | collective-permute-start | bytes 1769480 | tf_op jit(solution)/shard_map/ppermute | solution.py:38
  74.8 13.8 %all_to_all.5 = bf16[16,16,384]{2,1,0:T(8,128)(2,1)} all-to-all(bf16[16,16,384]{2,1,0:T(8,128)(2,1)S(1)} %get-tuple-element.43), channel_id=1, replica_groups=mesh['y'=4,'x'=4,'core'=2,'mp'=8] {'y','x'}, dimensions={0} | all-to-all | bytes 393216 | tf_op jit(solution)/shard_map/all_to_all | solution.py:481
  88.7 5.0 %shard_map.81 = (f32[96,1152]{1,0:T(8,128)S(1)}, f32[96,1152]{1,0:T(8,128)S(1)}) custom-call(bf16[96,3072]{1,0:T(8,128)(2,1)S(1)} %get-tuple-element.46.own_ref, bf16[96,3072]{1,0:T(8,128)(2,1)S(1)} %collective-permute-done.9.other_ref, bf16[16,3,192,384]{3,2,1,0:T(8,128)(2,1)} %bitcast.12), custom_call_target="tpu_custom_call" | custom-call | flops 1360000000 | bytes 9000000 | tf_op jit(solution)/shard_map/pallas_call | solution.py:246
  96.3 2.4 %shard_map.82.refs_0_ = bf16[112,1152]{1,0:T(8,128)(2,1)S(1)} custom-call(f32[96,1152]{1,0:T(8,128)S(1)} %get-tuple-element.48.raw_ref, f32[96,1152]{1,0:T(8,128)S(1)} %collective-permute-done.10.more_ref, s32[96,128]{1,0:T(8,128)S(1)} %get-tuple-element.50.row_ref, s32[8,96]{1,0:T(8,128)S(1)} %get-tuple-element.51.column_ref, ...), custom_call_target="tpu_custom_call" | custom-call | flops 50000000 | bytes 1500000 | tf_op jit(solution)/shard_map/pallas_call | solution.py:329
  98.8 2.7 %collective-permute-start.12 = (bf16[112,1152]{1,0:T(8,128)(2,1)S(1)}, bf16[112,1152]{1,0:T(8,128)(2,1)S(1)}, u32[]{:S(2)}, u32[]{:S(2)}) collective-permute-start(bf16[112,1152]{1,0:T(8,128)(2,1)S(1)} %shard_map.82.refs_0_), channel_id=1, source_target_pairs={{0,48},{8,200},{16,0},{24,216},{32,16},{40,232},{48,32},{56,248},{... | collective-permute-start | bytes 774152 | tf_op jit(solution)/shard_map/ppermute | solution.py:50
  101.5 4.1 %collective-permute-done.11.refs_1_ = bf16[112,1152]{1,0:T(8,128)(2,1)S(1)} collective-permute-done((bf16[112,1152]{1,0:T(8,128)(2,1)S(1)}, bf16[112,1152]{1,0:T(8,128)(2,1)S(1)}, u32[]{:S(2)}, u32[]{:S(2)}) %collective-permute-start.11) | collective-permute-done | bytes 258080 | tf_op jit(solution)/shard_map/ppermute | solution.py:50
  105.6 1.9 %collective-permute-done.12.refs_2_ = bf16[112,1152]{1,0:T(8,128)(2,1)S(1)} collective-permute-done((bf16[112,1152]{1,0:T(8,128)(2,1)S(1)}, bf16[112,1152]{1,0:T(8,128)(2,1)S(1)}, u32[]{:S(2)}, u32[]{:S(2)}) %collective-permute-start.12) | collective-permute-done | bytes 258080 | tf_op jit(solution)/shard_map/ppermute | solution.py:50
  108.6 2.7 %collective-permute-start.15 = (bf16[384,1152]{1,0:T(8,128)(2,1)S(1)}, bf16[384,1152]{1,0:T(8,128)(2,1)S(1)}, u32[]{:S(2)}, u32[]{:S(2)}) collective-permute-start(bf16[384,1152]{1,0:T(8,128)(2,1)S(1)} %get-tuple-element.58.refs_0_), channel_id=1, source_target_pairs={{0,192},{8,56},{16,208},{24,8},{32,224},{40,24},{48,240},{56,40},{... | collective-permute-start | bytes 2654216 | tf_op jit(solution)/shard_map/ppermute | solution.py:50
  111.3 3.5 %collective-permute-start.17 = (f32[8,128]{1,0:T(8,128)S(1)}, f32[8,128]{1,0:T(8,128)S(1)}, u32[]{:S(2)}, u32[]{:S(2)}) collective-permute-start(f32[8,128]{1,0:T(8,128)S(1)} %get-tuple-element.59), channel_id=1, source_target_pairs={{0,2},{1,3},{2,4},{3,5},{4,6},{5,7},{6,0},{7,1},{8,10},{9,11},{10,... | collective-permute-start | bytes 12296 | tf_op jit(solution)/shard_map/ppermute | solution.py:34
  116.7 3.8 %collective-permute-done.18 = f32[8,128]{1,0:T(8,128)S(1)} collective-permute-done((f32[8,128]{1,0:T(8,128)S(1)}, f32[8,128]{1,0:T(8,128)S(1)}, u32[]{:S(2)}, u32[]{:S(2)}) %collective-permute-start.18) | collective-permute-done | bytes 4128 | tf_op jit(solution)/shard_map/ppermute | solution.py:34
  120.4 2.7 %collective-permute-done.19 = f32[8,128]{1,0:T(8,128)S(1)} collective-permute-done((f32[8,128]{1,0:T(8,128)S(1)}, f32[8,128]{1,0:T(8,128)S(1)}, u32[]{:S(2)}, u32[]{:S(2)}) %collective-permute-start.19) | collective-permute-done | bytes 4128 | tf_op jit(solution)/shard_map/ppermute | solution.py:50
  123.3 3.5 %collective-permute-start.21 = (f32[8,128]{1,0:T(8,128)S(1)}, f32[8,128]{1,0:T(8,128)S(1)}, u32[]{:S(2)}, u32[]{:S(2)}) collective-permute-start(f32[8,128]{1,0:T(8,128)S(1)} %add.21), channel_id=1, source_target_pairs={{0,4},{1,5},{2,6},{3,7},{4,0},{5,1},{6,2},{7,3},{8,12},{9,13},{10,... | collective-permute-start | bytes 12296 | tf_op jit(solution)/shard_map/ppermute | solution.py:34
  129.7 3.6 %collective-permute-start.22 = (f32[8,128]{1,0:T(8,128)S(1)}, f32[8,128]{1,0:T(8,128)S(1)}, u32[]{:S(2)}, u32[]{:S(2)}) collective-permute-start(f32[8,128]{1,0:T(8,128)S(1)} %add.22), channel_id=1, source_target_pairs={{0,128},{8,40},{16,144},{24,56},{32,160},{40,8},{48,176},{56,24},{... | collective-permute-start | bytes 12296 | tf_op jit(solution)/shard_map/ppermute | solution.py:50
  137.1 6.0 %collective-permute-start.23 = (f32[3,192,384]{2,1,0:T(8,128)S(1)}, f32[3,192,384]{2,1,0:T(8,128)S(1)}, u32[]{:S(2)}, u32[]{:S(2)}) collective-permute-start(f32[3,192,384]{2,1,0:T(8,128)S(1)} %shard_map.86), channel_id=1, source_target_pairs={{0,8},{8,0},{1,9},{9,1},{2,10},{10,2},{3,11},{11,3},{4,12},{12,4},... | collective-permute-start | bytes 2654216 | tf_op jit(solution)/shard_map/ppermute | solution.py:38
  (59 shorter events, 23.9 us)
Async XLA Ops:
  7.2 81.5 %all-gather.7.cloned.1.call-start = ((), (), s32[]{:S(2)}) async-start(), calls=%async_computation.2 | async-start | bytes 7520256 | tf_op jit(solution)/shard_map/all_gather | solution.py:472
  7.9 119.0 %all-gather.5.cloned.1.call-start = ((), (), s32[]{:S(2)}) async-start(), calls=%async_computation.1 | async-start | bytes 1769472 | tf_op jit(solution)/shard_map/all_gather | solution.py:483
  10.5 30.4 %collective-permute-start = (bf16[64,1024]{1,0:T(8,128)(2,1)}, bf16[64,1024]{1,0:T(8,128)(2,1)S(1)}, u32[]{:S(2)}, u32[]{:S(2)}) collective-permute-start(bf16[64,1024]{1,0:T(8,128)(2,1)} %get-tuple-element.39), channel_id=1, source_target_pairs={{128,0},{136,8},{144,16},{152,24},{160,32},{168,40},{176,48},{184,... | collective-permute-start | bytes 393224 | tf_op jit(solution)/shard_map/ppermute | solution.py:477
  43.6 9.9 %collective-permute-start.1 = (bf16[96,768]{1,0:T(8,128)(2,1)S(1)}, bf16[96,768]{1,0:T(8,128)(2,1)S(1)}, u32[]{:S(2)}, u32[]{:S(2)}) collective-permute-start(bf16[96,768]{1,0:T(8,128)(2,1)S(1)} %get-tuple-element.41.refs_0_), channel_id=1, source_target_pairs={{0,1},{1,2},{2,3},{3,4},{4,5},{5,6},{6,7},{7,0},{8,9},{9,10},{10,1... | collective-permute-start | bytes 442376 | tf_op jit(solution)/shard_map/ppermute | solution.py:34
  45.3 8.2 %collective-permute-start.2 = (bf16[96,768]{1,0:T(8,128)(2,1)S(1)}, bf16[96,768]{1,0:T(8,128)(2,1)S(1)}, u32[]{:S(2)}, u32[]{:S(2)}) collective-permute-start(bf16[96,768]{1,0:T(8,128)(2,1)S(1)} %get-tuple-element.41.refs_0_), channel_id=1, source_target_pairs={{0,7},{1,0},{2,1},{3,2},{4,3},{5,4},{6,5},{7,6},{8,15},{9,8},{10,9... | collective-permute-start | bytes 442376 | tf_op jit(solution)/shard_map/ppermute | solution.py:34
  53.5 6.0 %collective-permute-start.3 = (bf16[96,768]{1,0:T(8,128)(2,1)S(1)}, bf16[96,768]{1,0:T(8,128)(2,1)S(1)}, u32[]{:S(2)}, u32[]{:S(2)}) collective-permute-start(bf16[96,768]{1,0:T(8,128)(2,1)S(1)} %collective-permute-done.1.refs_1_), channel_id=1, source_target_pairs={{0,1},{1,2},{2,3},{3,4},{4,5},{5,6},{6,7},{7,0},{8,9},{9,10},{10,1... | collective-permute-start | bytes 442376 | tf_op jit(solution)/shard_map/ppermute | solution.py:34
  53.5 6.0 %collective-permute-start.4 = (bf16[96,768]{1,0:T(8,128)(2,1)S(1)}, bf16[96,768]{1,0:T(8,128)(2,1)S(1)}, u32[]{:S(2)}, u32[]{:S(2)}) collective-permute-start(bf16[96,768]{1,0:T(8,128)(2,1)S(1)} %collective-permute-done.2.refs_2_), channel_id=1, source_target_pairs={{0,7},{1,0},{2,1},{3,2},{4,3},{5,4},{6,5},{7,6},{8,15},{9,8},{10,9... | collective-permute-start | bytes 442376 | tf_op jit(solution)/shard_map/ppermute | solution.py:34
  59.5 5.6 %collective-permute-start.5 = (bf16[96,768]{1,0:T(8,128)(2,1)S(1)}, bf16[96,768]{1,0:T(8,128)(2,1)S(1)}, u32[]{:S(2)}, u32[]{:S(2)}) collective-permute-start(bf16[96,768]{1,0:T(8,128)(2,1)S(1)} %collective-permute-done.3.refs_3_), channel_id=1, source_target_pairs={{0,1},{1,2},{2,3},{3,4},{4,5},{5,6},{6,7},{7,0},{8,9},{9,10},{10,1... | collective-permute-start | bytes 442376 | tf_op jit(solution)/shard_map/ppermute | solution.py:34
  59.5 5.6 %collective-permute-start.6 = (bf16[96,768]{1,0:T(8,128)(2,1)S(1)}, bf16[96,768]{1,0:T(8,128)(2,1)S(1)}, u32[]{:S(2)}, u32[]{:S(2)}) collective-permute-start(bf16[96,768]{1,0:T(8,128)(2,1)S(1)} %collective-permute-done.4.refs_4_), channel_id=1, source_target_pairs={{0,7},{1,0},{2,1},{3,2},{4,3},{5,4},{6,5},{7,6},{8,15},{9,8},{10,9... | collective-permute-start | bytes 442376 | tf_op jit(solution)/shard_map/ppermute | solution.py:34
  65.1 4.8 %collective-permute-start.7 = (bf16[48,768]{1,0:T(8,128)(2,1)S(1)}, bf16[48,768]{1,0:T(8,128)(2,1)S(1)}, u32[]{:S(2)}, u32[]{:S(2)}) collective-permute-start(bf16[48,768]{1,0:T(8,128)(2,1)S(1)} %slice.8), channel_id=1, source_target_pairs={{0,1},{1,2},{2,3},{3,4},{4,5},{5,6},{6,7},{7,0},{8,9},{9,10},{10,1... | collective-permute-start | bytes 221192 | tf_op jit(solution)/shard_map/ppermute | solution.py:34
  65.1 4.8 %collective-permute-start.8 = (bf16[48,768]{1,0:T(8,128)(2,1)S(1)}, bf16[48,768]{1,0:T(8,128)(2,1)S(1)}, u32[]{:S(2)}, u32[]{:S(2)}) collective-permute-start(bf16[48,768]{1,0:T(8,128)(2,1)S(1)} %slice.9), channel_id=1, source_target_pairs={{0,7},{1,0},{2,1},{3,2},{4,3},{5,4},{6,5},{7,6},{8,15},{9,8},{10,9... | collective-permute-start | bytes 221192 | tf_op jit(solution)/shard_map/ppermute | solution.py:34
  71.7 16.9 %collective-permute-start.9 = (bf16[96,3072]{1,0:T(8,128)(2,1)S(1)}, bf16[96,3072]{1,0:T(8,128)(2,1)S(1)}, u32[]{:S(2)}, u32[]{:S(2)}) collective-permute-start(bf16[96,3072]{1,0:T(8,128)(2,1)S(1)} %get-tuple-element.42), channel_id=1, source_target_pairs={{0,8},{8,0},{1,9},{9,1},{2,10},{10,2},{3,11},{11,3},{4,12},{12,4},... | collective-permute-start | bytes 1769480 | tf_op jit(solution)/shard_map/ppermute | solution.py:38
  98.7 6.9 %collective-permute-start.11 = (bf16[112,1152]{1,0:T(8,128)(2,1)S(1)}, bf16[112,1152]{1,0:T(8,128)(2,1)S(1)}, u32[]{:S(2)}, u32[]{:S(2)}) collective-permute-start(bf16[112,1152]{1,0:T(8,128)(2,1)S(1)} %shard_map.82.refs_0_), channel_id=1, source_target_pairs={{0,16},{8,72},{16,32},{24,88},{32,48},{40,104},{48,0},{56,120},{64... | collective-permute-start | bytes 774152 | tf_op jit(solution)/shard_map/ppermute | solution.py:50
  98.8 8.7 %collective-permute-start.12 = (bf16[112,1152]{1,0:T(8,128)(2,1)S(1)}, bf16[112,1152]{1,0:T(8,128)(2,1)S(1)}, u32[]{:S(2)}, u32[]{:S(2)}) collective-permute-start(bf16[112,1152]{1,0:T(8,128)(2,1)S(1)} %shard_map.82.refs_0_), channel_id=1, source_target_pairs={{0,48},{8,200},{16,0},{24,216},{32,16},{40,232},{48,32},{56,248},{... | collective-permute-start | bytes 774152 | tf_op jit(solution)/shard_map/ppermute | solution.py:50
  101.5 7.0 %collective-permute-start.13 = (bf16[112,1152]{1,0:T(8,128)(2,1)S(1)}, bf16[112,1152]{1,0:T(8,128)(2,1)S(1)}, u32[]{:S(2)}, u32[]{:S(2)}) collective-permute-start(bf16[112,1152]{1,0:T(8,128)(2,1)S(1)} %shard_map.82.refs_0_), channel_id=1, source_target_pairs={{0,32},{8,136},{16,48},{24,152},{32,0},{40,168},{48,16},{56,184},{... | collective-permute-start | bytes 774152 | tf_op jit(solution)/shard_map/ppermute | solution.py:50
  108.5 14.6 %collective-permute-start.14 = (bf16[384,1152]{1,0:T(8,128)(2,1)S(1)}, bf16[384,1152]{1,0:T(8,128)(2,1)S(1)}, u32[]{:S(2)}, u32[]{:S(2)}) collective-permute-start(bf16[384,1152]{1,0:T(8,128)(2,1)S(1)} %get-tuple-element.58.refs_0_), channel_id=1, source_target_pairs={{0,64},{8,24},{16,80},{24,40},{32,96},{40,56},{48,112},{56,8},{64,... | collective-permute-start | bytes 2654216 | tf_op jit(solution)/shard_map/ppermute | solution.py:50
  108.6 14.6 %collective-permute-start.15 = (bf16[384,1152]{1,0:T(8,128)(2,1)S(1)}, bf16[384,1152]{1,0:T(8,128)(2,1)S(1)}, u32[]{:S(2)}, u32[]{:S(2)}) collective-permute-start(bf16[384,1152]{1,0:T(8,128)(2,1)S(1)} %get-tuple-element.58.refs_0_), channel_id=1, source_target_pairs={{0,192},{8,56},{16,208},{24,8},{32,224},{40,24},{48,240},{56,40},{... | collective-permute-start | bytes 2654216 | tf_op jit(solution)/shard_map/ppermute | solution.py:50
  111.3 4.9 %collective-permute-start.16 = (f32[8,128]{1,0:T(8,128)S(1)}, f32[8,128]{1,0:T(8,128)S(1)}, u32[]{:S(2)}, u32[]{:S(2)}) collective-permute-start(f32[8,128]{1,0:T(8,128)S(1)} %get-tuple-element.59), channel_id=1, source_target_pairs={{0,1},{1,2},{2,3},{3,4},{4,5},{5,6},{6,7},{7,0},{8,9},{9,10},{10,1... | collective-permute-start | bytes 12296 | tf_op jit(solution)/shard_map/ppermute | solution.py:34
  111.3 5.4 %collective-permute-start.17 = (f32[8,128]{1,0:T(8,128)S(1)}, f32[8,128]{1,0:T(8,128)S(1)}, u32[]{:S(2)}, u32[]{:S(2)}) collective-permute-start(f32[8,128]{1,0:T(8,128)S(1)} %get-tuple-element.59), channel_id=1, source_target_pairs={{0,2},{1,3},{2,4},{3,5},{4,6},{5,7},{6,0},{7,1},{8,10},{9,11},{10,... | collective-permute-start | bytes 12296 | tf_op jit(solution)/shard_map/ppermute | solution.py:34
  114.8 5.6 %collective-permute-start.18 = (f32[8,128]{1,0:T(8,128)S(1)}, f32[8,128]{1,0:T(8,128)S(1)}, u32[]{:S(2)}, u32[]{:S(2)}) collective-permute-start(f32[8,128]{1,0:T(8,128)S(1)} %get-tuple-element.59), channel_id=1, source_target_pairs={{0,3},{1,4},{2,5},{3,6},{4,7},{5,0},{6,1},{7,2},{8,11},{9,12},{10,... | collective-permute-start | bytes 12296 | tf_op jit(solution)/shard_map/ppermute | solution.py:34
  123.2 13.5 %collective-permute-start.20 = (bf16[384,1152]{1,0:T(8,128)(2,1)S(1)}, bf16[384,1152]{1,0:T(8,128)(2,1)S(1)}, u32[]{:S(2)}, u32[]{:S(2)}) collective-permute-start(bf16[384,1152]{1,0:T(8,128)(2,1)S(1)} %collective-permute-done.14.refs_1_), channel_id=1, source_target_pairs={{0,64},{8,24},{16,80},{24,40},{32,96},{40,56},{48,112},{56,8},{64,... | collective-permute-start | bytes 2654216 | tf_op jit(solution)/shard_map/ppermute | solution.py:50
  123.3 6.5 %collective-permute-start.21 = (f32[8,128]{1,0:T(8,128)S(1)}, f32[8,128]{1,0:T(8,128)S(1)}, u32[]{:S(2)}, u32[]{:S(2)}) collective-permute-start(f32[8,128]{1,0:T(8,128)S(1)} %add.21), channel_id=1, source_target_pairs={{0,4},{1,5},{2,6},{3,7},{4,0},{5,1},{6,2},{7,3},{8,12},{9,13},{10,... | collective-permute-start | bytes 12296 | tf_op jit(solution)/shard_map/ppermute | solution.py:34
  129.7 6.7 %collective-permute-start.22 = (f32[8,128]{1,0:T(8,128)S(1)}, f32[8,128]{1,0:T(8,128)S(1)}, u32[]{:S(2)}, u32[]{:S(2)}) collective-permute-start(f32[8,128]{1,0:T(8,128)S(1)} %add.22), channel_id=1, source_target_pairs={{0,128},{8,40},{16,144},{24,56},{32,160},{40,8},{48,176},{56,24},{... | collective-permute-start | bytes 12296 | tf_op jit(solution)/shard_map/ppermute | solution.py:50
  137.1 8.0 %collective-permute-start.23 = (f32[3,192,384]{2,1,0:T(8,128)S(1)}, f32[3,192,384]{2,1,0:T(8,128)S(1)}, u32[]{:S(2)}, u32[]{:S(2)}) collective-permute-start(f32[3,192,384]{2,1,0:T(8,128)S(1)} %shard_map.86), channel_id=1, source_target_pairs={{0,8},{8,0},{1,9},{9,1},{2,10},{10,2},{3,11},{11,3},{4,12},{12,4},... | collective-permute-start | bytes 2654216 | tf_op jit(solution)/shard_map/ppermute | solution.py:38
  (6 other events, 10.5 us)
Sparse Core Ops, SparseCore 0:
  10.4 76.0 all-gather.6
  88.8 35.6 all-gather.4
where the time goes:
time: 153 us
  starting transfers between devices  43.4 us (28%)
  blocking collectives  42.9 us (28%)
  waiting for transfers between devices  32 us (21%)
  Pallas kernels  17.3 us (11%)
  between operations  14.2 us (9%)
  local copies, waits for them, and re-layouts  3.07 us (2%)
    all_gather x1, blocking collectives, local(): wide = lax.all_gather(embed_part, DP, axis=0, tiled=True)  29.1 us
    ppermute x12, starting transfers between devices, shift(): lax.ppermute(array, axis, [(i, (i + step) % size) for i in range(size)])  22.5 us
    ppermute x12, waiting for transfers between devices, shift(): lax.ppermute(array, axis, [(i, (i + step) % size) for i in range(size)])  16.9 us
    all_to_all x1, blocking collectives, local(): lax.all_to_all(chip_blocks, ('y', 'x'), split_axis=0, concat_axis=0, tile...  13.8 us
    ppermute x8, waiting for transfers between devices, turn(): return lax.ppermute(array, DP, pairs)  11.4 us
    ppermute x4, starting transfers between devices, swap(): return lax.ppermute(array, 'core', [(0, 1), (1, 0)])  10.3 us
    ppermute x8, starting transfers between devices, turn(): return lax.ppermute(array, DP, pairs)  9.16 us
    pallas_call x1, Pallas kernels, project(): pl.pallas_call(project_kernel, grid=(chips // step,), out_shape=(jax.Shap...  4.97 us
  transfers between devices with their start and end apart: 27, of which 15 were waited for; matrix products, arithmetic and copies ran while one was open for 0% of the time, Pallas kernels for 10%

commit v1 on v0

--- a/solution.py
+++ b/solution.py
@@ -338,69 +338,50 @@
     )(raw, more, column, row, targets, patch_total)
 
 
-def turn_kernel(place_ref, blocks_ref, own_ref, other_ref):
+def first_kernel(place_ref, blocks_ref, *refs):
+    pieces, (own_out, other_out, own_last, other_last) = refs[:-4], refs[-4:]
     y, x, core = place_ref[0], place_ref[1], place_ref[2]
     half = blocks_ref.shape[3] // 2
-    rows = SHARES * SHARE
-    ring = (0, -1, 1, 2)
-    pieces = []
-    for far in ring:
-        for near in ring:
-            step_x = jnp.where(core == 0, near, far)
-            step_y = jnp.where(core == 0, far, near)
+    first = core == 0
+    totals = [None, None]
+    for index, far in enumerate((0, -1, 1, 2)):
+        several = []
+        for near in (0, -1, 1, 2):
+            step_x = jnp.where(first, near, far)
+            step_y = jnp.where(first, far, near)
             chip = lax.rem(y + step_y + SIDE, SIDE) * SIDE + lax.rem(x + step_x + SIDE, SIDE)
-            pieces += [blocks_ref[share, chip] for share in range(SHARES)]
-    for group in range(SIDE):
-        several = pieces[group * SIDE * SHARES : (group + 1) * SIDE * SHARES]
+            several += [blocks_ref[share, chip] for share in range(SHARES)]
         wide = jnp.concatenate(several, axis=0).astype(F32).T.astype(BF16)
-        columns = slice(group * SIDE * rows, (group + 1) * SIDE * rows)
-        first = core == 0
-        own_ref[:, columns] = jnp.where(first, wide[:half], wide[half:])
-        other_ref[:, columns] = jnp.where(first, wide[half:], wide[:half])
-
-
-def turn_blocks(blocks, place):
-    _, chips, _, feats = blocks.shape
-    return pl.pallas_call(
-        turn_kernel,
-        out_shape=(jax.ShapeDtypeStruct((feats // 2, chips * KEEP), BF16),) * 2,
-        in_specs=[SMEM, VMEM],
-        out_specs=(VMEM, VMEM),
-        compiler_params=ROOM,
-        cost_estimate=pl.CostEstimate(flops=1_000_000, bytes_accessed=2_400_000, transcendentals=0),
-    )(place, blocks)
-
-
-def grad_kernel(parts, own_ref, other_ref, *refs):
-    pieces, (own_out, other_out) = refs[:parts], refs[parts:]
-    for left_ref, out_ref in ((other_ref, other_out), (own_ref, own_out)):
-        groups, _, span = out_ref.shape
-        total = None
-        start = 0
-        for piece in pieces:
-            rows = piece.shape[0]
-            product = jnp.dot(
-                left_ref[:, start : start + rows], piece[...], preferred_element_type=F32
-            )
-            total = product if total is None else total + product
-            start += rows
+        own = jnp.where(first, wide[:half], wide[half:])
+        other = jnp.where(first, wide[half:], wide[:half])
+        if index == len(pieces):
+            own_last[...] = own
+            other_last[...] = other
+            continue
+        for side, left in enumerate((own, other)):
+            product = jnp.dot(left, pieces[index][...], preferred_element_type=F32)
+            totals[side] = product if totals[side] is None else totals[side] + product
+    groups, _, span = own_out.shape
+    for total, out_ref in zip(totals, (own_out, other_out)):
         for group in range(groups):
             out_ref[group] = total[:, group * span : (group + 1) * span]
 
 
-def grad_first(own, other, pieces, groups):
-    width = pieces[0].shape[1]
-    part = jax.ShapeDtypeStruct((groups, own.shape[0], width // groups), F32)
-    return pl.pallas_call(
-        functools.partial(grad_kernel, len(pieces)),
-        out_shape=(part, part),
-        in_specs=[VMEM] * (2 + len(pieces)),
-        out_specs=(VMEM, VMEM),
+def grad_first(place, blocks, pieces, groups):
+    depth, width = pieces[0].shape
+    feats = blocks.shape[3] // 2
+    part = jax.ShapeDtypeStruct((groups, feats, width // groups), F32)
+    last = jax.ShapeDtypeStruct((feats, depth), BF16)
+    return pl.pallas_call(
+        first_kernel,
+        out_shape=(part, part, last, last),
+        in_specs=[SMEM] + [VMEM] * (1 + len(pieces)),
+        out_specs=(VMEM,) * 4,
         compiler_params=ROOM,
         cost_estimate=pl.CostEstimate(
-            flops=1_000_000_000, bytes_accessed=5_000_000, transcendentals=0
-        ),
-    )(own, other, *pieces)
+            flops=1_000_000_000, bytes_accessed=6_000_000, transcendentals=0
+        ),
+    )(place, blocks, *pieces)
 
 
 def last_kernel(start, left_ref, piece_ref, part_ref, out_ref):
@@ -410,13 +391,14 @@
     )
     groups, _, span = out_ref.shape
     for group in range(groups):
-        out_ref[group] = part_ref[group] + product[:, group * span : (group + 1) * span]
-
-
-def grad_last(left, piece, part):
+        whole = part_ref[group] + product[:, group * span : (group + 1) * span]
+        out_ref[group] = whole.astype(out_ref.dtype)
+
+
+def grad_last(left, piece, part, dtype):
     return pl.pallas_call(
         functools.partial(last_kernel, left.shape[1] - piece.shape[0]),
-        out_shape=jax.ShapeDtypeStruct(part.shape, F32),
+        out_shape=jax.ShapeDtypeStruct(part.shape, dtype),
         in_specs=[VMEM] * 3,
         out_specs=VMEM,
         compiler_params=ROOM,
@@ -427,7 +409,7 @@
 
 
 def finish_kernel(a_ref, b_ref, sum_ref, more_ref, total_ref, out_ref, loss_ref):
-    out_ref[...] = a_ref[...] + b_ref[...]
+    out_ref[...] = a_ref[...] + b_ref[...].astype(F32)
     squared = sum_ref[:1, :1] + more_ref[:1, :1]
     loss_ref[...] = squared / (2.0 * total_ref[:1, :1])
 
@@ -501,17 +483,18 @@
     opposite = turn(behind, False, 1)
     tile = tile + shift(tile, "mp", N_MP, 4)
     tile = tile + turn(tile, False, -2)
-    own_left, other_left = turn_blocks(chip_rows, jnp.stack([y, x, core]))
     groups = project_weight.shape[1]
-    own_grad, other_grad = grad_first(own_left, other_left, (near, behind, ahead), groups)
+    own_grad, other_grad, own_left, other_left = grad_first(
+        jnp.stack([y, x, core]), chip_rows, (near, behind, ahead), groups
+    )
     opposite, tile, own_grad, other_grad = lax.optimization_barrier(
         (opposite, tile, own_grad, other_grad)
     )
     more_grad, more_tile = lax.optimization_barrier(
-        (swap(grad_last(other_left, opposite, other_grad)), swap(tile))
+        (swap(grad_last(other_left, opposite, other_grad, BF16)), swap(tile))
     )
     weight_grad, loss_tile = finish(
-        grad_last(own_left, opposite, own_grad), more_grad, tile, more_tile, total_tile
+        grad_last(own_left, opposite, own_grad, F32), more_grad, tile, more_tile, total_tile
     )
     loss_value = loss_tile[0, 0]
     return (weight_grad.transpose(1, 0, 2), loss_value)

time: 153 us -> 153 us (level)
    ppermute x12, waiting for transfers between devices: 16.9 us -> 19.2 us  [shift(): lax.ppermute(array, axis, [(i, (i + step) % size) for i in range(size)])]
    unnamed x6 -> x4, local copies, waits for them, and re-layouts: 3.06 us -> 1.65 us
    pallas_call x2 -> x1, Pallas kernels: 2.6 us -> 3.16 us  [grad_first(): pl.pallas_call(first_kernel, out_shape=(part, part, last, last), in_specs...]
  transfers between devices with their start and end apart: 27 -> 27, of which waited for: 15 -> 15; matrix products, arithmetic and copies ran while one was open for 0% -> 0% of each run, Pallas kernels for 10% -> 11%
where the time goes in v1:
time: 153 us; the launch traced here: 152 us
  blocking collectives  43 us (28%)
  starting transfers between devices  42.3 us (28%)
  waiting for transfers between devices  33.1 us (22%)
  Pallas kernels  17.8 us (12%)
  between operations  14.2 us (9%)
  local copies, waits for them, and re-layouts  1.66 us (1%)
    all_gather x1, blocking collectives, local(): wide = lax.all_gather(embed_part, DP, axis=0, tiled=True)  29.1 us
    ppermute x12, starting transfers between devices, shift(): lax.ppermute(array, axis, [(i, (i + step) % size) for i in range(size)])  22.4 us
    ppermute x12, waiting for transfers between devices, shift(): lax.ppermute(array, axis, [(i, (i + step) % size) for i in range(size)])  19.2 us
    all_to_all x1, blocking collectives, local(): lax.all_to_all(chip_blocks, ('y', 'x'), split_axis=0, concat_axis=0, tile...  13.9 us
    ppermute x8, waiting for transfers between devices, turn(): return lax.ppermute(array, DP, pairs)  10.8 us
    ppermute x4, starting transfers between devices, swap(): return lax.ppermute(array, 'core', [(0, 1), (1, 0)])  10.3 us
    ppermute x8, starting transfers between devices, turn(): return lax.ppermute(array, DP, pairs)  8.21 us
    pallas_call x1, Pallas kernels, project(): pl.pallas_call(project_kernel, grid=(chips // step,), out_shape=(jax.Shap...  4.97 us
  transfers between devices with their start and end apart: 27, of which 15 were waited for; matrix products, arithmetic and copies ran while one was open for 0% of the time, Pallas kernels for 11%

profile of v1, /device:TPU:1, one launch (start us, length us, event | category | flops | bytes accessed | tf_op | source)
XLA Modules:
  0.0 152.3 jit_solution(5645486914534989984)
XLA Ops:
  7.9 2.6 %shard_map.77 = (bf16[192,1024]{1,0:T(8,128)(2,1)}, bf16[64,1024]{1,0:T(8,128)(2,1)}, bf16[24,640]{1,0:T(8,128)(2,1)}) custom-call(s32[8]{0:T(128)} %counts_ref.3, bf16[588,128]{1,0:T(8,128)(2,1)} %bitcast.14, bf16[128,384]{1,0:T(8,128)(2,1)} %refs_1_.1, s32[1,128]{1,0:T(1,128)} %bitcast.15, bf16[24,588]{1,0:T(8,128)(2,1)} %refs_3_.1), custom_call_target="tpu_custom_call" | custom-call | flops 1000000 | bytes 1000000 | tf_op jit(solution)/shard_map/pallas_call | solution.py:94
  11.8 29.1 %all_gather.15.wide_ref = bf16[768,640]{1,0:T(8,128)(2,1)S(1)} all-gather(bf16[24,640]{1,0:T(8,128)(2,1)} %get-tuple-element.40), channel_id=1, replica_groups=mesh['y'=4,'x'=4,'core'=2,'mp'=8] {'y','x','core'}, dimensions={0}, use_global_device_ids=true | all-gather | bytes 1013760 | tf_op jit(solution)/shard_map/all_gather | solution.py:460
  45.3 4.1 %collective-permute-start.2 = (bf16[96,768]{1,0:T(8,128)(2,1)S(1)}, bf16[96,768]{1,0:T(8,128)(2,1)S(1)}, u32[]{:S(2)}, u32[]{:S(2)}) collective-permute-start(bf16[96,768]{1,0:T(8,128)(2,1)S(1)} %get-tuple-element.41.refs_0_), channel_id=1, source_target_pairs={{0,7},{1,0},{2,1},{3,2},{4,3},{5,4},{6,5},{7,6},{8,15},{9,8},{10,9... | collective-permute-start | bytes 442376 | tf_op jit(solution)/shard_map/ppermute | solution.py:34
  49.4 4.0 %collective-permute-done.1.refs_1_ = bf16[96,768]{1,0:T(8,128)(2,1)S(1)} collective-permute-done((bf16[96,768]{1,0:T(8,128)(2,1)S(1)}, bf16[96,768]{1,0:T(8,128)(2,1)S(1)}, u32[]{:S(2)}, u32[]{:S(2)}) %collective-permute-start.1) | collective-permute-done | bytes 147488 | tf_op jit(solution)/shard_map/ppermute | solution.py:34
  53.4 2.7 %collective-permute-start.4 = (bf16[96,768]{1,0:T(8,128)(2,1)S(1)}, bf16[96,768]{1,0:T(8,128)(2,1)S(1)}, u32[]{:S(2)}, u32[]{:S(2)}) collective-permute-start(bf16[96,768]{1,0:T(8,128)(2,1)S(1)} %collective-permute-done.2.refs_2_), channel_id=1, source_target_pairs={{0,7},{1,0},{2,1},{3,2},{4,3},{5,4},{6,5},{7,6},{8,15},{9,8},{10,9... | collective-permute-start | bytes 442376 | tf_op jit(solution)/shard_map/ppermute | solution.py:34
  56.1 3.3 %collective-permute-done.3.refs_3_ = bf16[96,768]{1,0:T(8,128)(2,1)S(1)} collective-permute-done((bf16[96,768]{1,0:T(8,128)(2,1)S(1)}, bf16[96,768]{1,0:T(8,128)(2,1)S(1)}, u32[]{:S(2)}, u32[]{:S(2)}) %collective-permute-start.3) | collective-permute-done | bytes 147488 | tf_op jit(solution)/shard_map/ppermute | solution.py:34
  59.3 2.7 %collective-permute-start.6 = (bf16[96,768]{1,0:T(8,128)(2,1)S(1)}, bf16[96,768]{1,0:T(8,128)(2,1)S(1)}, u32[]{:S(2)}, u32[]{:S(2)}) collective-permute-start(bf16[96,768]{1,0:T(8,128)(2,1)S(1)} %collective-permute-done.4.refs_4_), channel_id=1, source_target_pairs={{0,7},{1,0},{2,1},{3,2},{4,3},{5,4},{6,5},{7,6},{8,15},{9,8},{10,9... | collective-permute-start | bytes 442376 | tf_op jit(solution)/shard_map/ppermute | solution.py:34
  62.0 2.9 %collective-permute-done.5.refs_5_ = bf16[96,768]{1,0:T(8,128)(2,1)S(1)} collective-permute-done((bf16[96,768]{1,0:T(8,128)(2,1)S(1)}, bf16[96,768]{1,0:T(8,128)(2,1)S(1)}, u32[]{:S(2)}, u32[]{:S(2)}) %collective-permute-start.5) | collective-permute-done | bytes 147488 | tf_op jit(solution)/shard_map/ppermute | solution.py:34
  65.0 2.7 %collective-permute-start.8 = (bf16[48,768]{1,0:T(8,128)(2,1)S(1)}, bf16[48,768]{1,0:T(8,128)(2,1)S(1)}, u32[]{:S(2)}, u32[]{:S(2)}) collective-permute-start(bf16[48,768]{1,0:T(8,128)(2,1)S(1)} %slice.9), channel_id=1, source_target_pairs={{0,7},{1,0},{2,1},{3,2},{4,3},{5,4},{6,5},{7,6},{8,15},{9,8},{10,9... | collective-permute-start | bytes 221192 | tf_op jit(solution)/shard_map/ppermute | solution.py:34
  71.6 3.1 %collective-permute-start.9 = (bf16[96,3072]{1,0:T(8,128)(2,1)S(1)}, bf16[96,3072]{1,0:T(8,128)(2,1)S(1)}, u32[]{:S(2)}, u32[]{:S(2)}) collective-permute-start(bf16[96,3072]{1,0:T(8,128)(2,1)S(1)} %get-tuple-element.42), channel_id=1, source_target_pairs={{0,8},{8,0},{1,9},{9,1},{2,10},{10,2},{3,11},{11,3},{4,12},{12,4},... | collective-permute-start | bytes 1769480 | tf_op jit(solution)/shard_map/ppermute | solution.py:38
  74.7 13.9 %all_to_all.5 = bf16[16,16,384]{2,1,0:T(8,128)(2,1)} all-to-all(bf16[16,16,384]{2,1,0:T(8,128)(2,1)S(1)} %get-tuple-element.43), channel_id=1, replica_groups=mesh['y'=4,'x'=4,'core'=2,'mp'=8] {'y','x'}, dimensions={0} | all-to-all | bytes 393216 | tf_op jit(solution)/shard_map/all_to_all | solution.py:463
  88.7 5.0 %shard_map.80 = (f32[96,1152]{1,0:T(8,128)S(1)}, f32[96,1152]{1,0:T(8,128)S(1)}) custom-call(bf16[96,3072]{1,0:T(8,128)(2,1)S(1)} %get-tuple-element.45.own_ref, bf16[96,3072]{1,0:T(8,128)(2,1)S(1)} %collective-permute-done.9.other_ref, bf16[16,3,192,384]{3,2,1,0:T(8,128)(2,1)} %bitcast.11), custom_call_target="tpu_custom_call" | custom-call | flops 1360000000 | bytes 9000000 | tf_op jit(solution)/shard_map/pallas_call | solution.py:246
  96.3 2.4 %shard_map.81.refs_0_ = bf16[112,1152]{1,0:T(8,128)(2,1)S(1)} custom-call(f32[96,1152]{1,0:T(8,128)S(1)} %get-tuple-element.47.raw_ref, f32[96,1152]{1,0:T(8,128)S(1)} %collective-permute-done.10.more_ref, s32[96,128]{1,0:T(8,128)S(1)} %get-tuple-element.49.row_ref, s32[8,96]{1,0:T(8,128)S(1)} %get-tuple-element.50.column_ref, ...), custom_call_target="tpu_custom_call" | custom-call | flops 50000000 | bytes 1500000 | tf_op jit(solution)/shard_map/pallas_call | solution.py:329
  98.8 2.7 %collective-permute-start.12 = (bf16[112,1152]{1,0:T(8,128)(2,1)S(1)}, bf16[112,1152]{1,0:T(8,128)(2,1)S(1)}, u32[]{:S(2)}, u32[]{:S(2)}) collective-permute-start(bf16[112,1152]{1,0:T(8,128)(2,1)S(1)} %shard_map.81.refs_0_), channel_id=1, source_target_pairs={{0,48},{8,200},{16,0},{24,216},{32,16},{40,232},{48,32},{56,248},{... | collective-permute-start | bytes 774152 | tf_op jit(solution)/shard_map/ppermute | solution.py:50
  101.5 4.1 %collective-permute-done.11.refs_1_ = bf16[112,1152]{1,0:T(8,128)(2,1)S(1)} collective-permute-done((bf16[112,1152]{1,0:T(8,128)(2,1)S(1)}, bf16[112,1152]{1,0:T(8,128)(2,1)S(1)}, u32[]{:S(2)}, u32[]{:S(2)}) %collective-permute-start.11) | collective-permute-done | bytes 258080 | tf_op jit(solution)/shard_map/ppermute | solution.py:50
  108.6 2.7 %collective-permute-start.15 = (bf16[384,1152]{1,0:T(8,128)(2,1)S(1)}, bf16[384,1152]{1,0:T(8,128)(2,1)S(1)}, u32[]{:S(2)}, u32[]{:S(2)}) collective-permute-start(bf16[384,1152]{1,0:T(8,128)(2,1)S(1)} %get-tuple-element.57.refs_0_), channel_id=1, source_target_pairs={{0,192},{8,56},{16,208},{24,8},{32,224},{40,24},{48,240},{56,40},{... | collective-permute-start | bytes 2654216 | tf_op jit(solution)/shard_map/ppermute | solution.py:50
  111.3 3.5 %collective-permute-start.17 = (f32[8,128]{1,0:T(8,128)S(1)}, f32[8,128]{1,0:T(8,128)S(1)}, u32[]{:S(2)}, u32[]{:S(2)}) collective-permute-start(f32[8,128]{1,0:T(8,128)S(1)} %get-tuple-element.58), channel_id=1, source_target_pairs={{0,2},{1,3},{2,4},{3,5},{4,6},{5,7},{6,0},{7,1},{8,10},{9,11},{10,... | collective-permute-start | bytes 12296 | tf_op jit(solution)/shard_map/ppermute | solution.py:34
  116.7 3.8 %collective-permute-done.18 = f32[8,128]{1,0:T(8,128)S(1)} collective-permute-done((f32[8,128]{1,0:T(8,128)S(1)}, f32[8,128]{1,0:T(8,128)S(1)}, u32[]{:S(2)}, u32[]{:S(2)}) %collective-permute-start.18) | collective-permute-done | bytes 4128 | tf_op jit(solution)/shard_map/ppermute | solution.py:34
  120.4 2.7 %collective-permute-done.19 = f32[8,128]{1,0:T(8,128)S(1)} collective-permute-done((f32[8,128]{1,0:T(8,128)S(1)}, f32[8,128]{1,0:T(8,128)S(1)}, u32[]{:S(2)}, u32[]{:S(2)}) %collective-permute-start.19) | collective-permute-done | bytes 4128 | tf_op jit(solution)/shard_map/ppermute | solution.py:50
  123.3 3.5 %collective-permute-start.21 = (f32[8,128]{1,0:T(8,128)S(1)}, f32[8,128]{1,0:T(8,128)S(1)}, u32[]{:S(2)}, u32[]{:S(2)}) collective-permute-start(f32[8,128]{1,0:T(8,128)S(1)} %add.21), channel_id=1, source_target_pairs={{0,4},{1,5},{2,6},{3,7},{4,0},{5,1},{6,2},{7,3},{8,12},{9,13},{10,... | collective-permute-start | bytes 12296 | tf_op jit(solution)/shard_map/ppermute | solution.py:34
  126.9 2.9 %collective-permute-done.21 = f32[8,128]{1,0:T(8,128)S(1)} collective-permute-done((f32[8,128]{1,0:T(8,128)S(1)}, f32[8,128]{1,0:T(8,128)S(1)}, u32[]{:S(2)}, u32[]{:S(2)}) %collective-permute-start.21) | collective-permute-done | bytes 4128 | tf_op jit(solution)/shard_map/ppermute | solution.py:34
  129.7 2.6 %collective-permute-start.22 = (f32[8,128]{1,0:T(8,128)S(1)}, f32[8,128]{1,0:T(8,128)S(1)}, u32[]{:S(2)}, u32[]{:S(2)}) collective-permute-start(f32[8,128]{1,0:T(8,128)S(1)} %add.22), channel_id=1, source_target_pairs={{0,128},{8,40},{16,144},{24,56},{32,160},{40,8},{48,176},{56,24},{... | collective-permute-start | bytes 12296 | tf_op jit(solution)/shard_map/ppermute | solution.py:50
  132.4 3.2 %shard_map.83 = (f32[3,192,384]{2,1,0:T(8,128)S(1)}, f32[3,192,384]{2,1,0:T(8,128)S(1)}, bf16[192,384]{1,0:T(8,128)(2,1)S(1)}, bf16[192,384]{1,0:T(8,128)(2,1)S(1)}) custom-call(s32[3]{0:T(128)S(1)} %pad_add_fusion.place_ref, bf16[8,16,16,384]{3,2,1,0:T(8,128)(2,1)} %bitcast.12, bf16[384,1152]{1,0:T(8,128)(2,1)S(1)} %get-tuple-element.57.refs_0_, ...), custom_call_target="tpu_custom_call" | custom-call | flops 1000000000 | bytes 6000000 | tf_op jit(solution)/shard_map/pallas_call | solution.py:375
  137.1 6.0 %collective-permute-start.23 = (bf16[3,192,384]{2,1,0:T(8,128)(2,1)S(1)}, bf16[3,192,384]{2,1,0:T(8,128)(2,1)S(1)}, u32[]{:S(2)}, u32[]{:S(2)}) collective-permute-start(bf16[3,192,384]{2,1,0:T(8,128)(2,1)S(1)} %shard_map.85), channel_id=1, source_target_pairs={{0,8},{8,0},{1,9},{9,1},{2,10},{10,2},{3,11},{11,3},{4,12},{12,4},... | collective-permute-start | bytes 1327112 | tf_op jit(solution)/shard_map/ppermute | solution.py:38
  (56 shorter events, 22.1 us)
Async XLA Ops:
  7.2 81.5 %all-gather.7.cloned.1.call-start = ((), (), s32[]{:S(2)}) async-start(), calls=%async_computation.2 | async-start | bytes 7520256 | tf_op jit(solution)/shard_map/all_gather | solution.py:454
  7.9 124.5 %all-gather.5.cloned.1.call-start = ((), (), s32[]{:S(2)}) async-start(), calls=%async_computation.1 | async-start | bytes 1769472 | tf_op jit(solution)/shard_map/all_gather | solution.py:465
  10.5 30.4 %collective-permute-start = (bf16[64,1024]{1,0:T(8,128)(2,1)}, bf16[64,1024]{1,0:T(8,128)(2,1)S(1)}, u32[]{:S(2)}, u32[]{:S(2)}) collective-permute-start(bf16[64,1024]{1,0:T(8,128)(2,1)} %get-tuple-element.39), channel_id=1, source_target_pairs={{128,0},{136,8},{144,16},{152,24},{160,32},{168,40},{176,48},{184,... | collective-permute-start | bytes 393224 | tf_op jit(solution)/shard_map/ppermute | solution.py:459
  43.6 9.8 %collective-permute-start.1 = (bf16[96,768]{1,0:T(8,128)(2,1)S(1)}, bf16[96,768]{1,0:T(8,128)(2,1)S(1)}, u32[]{:S(2)}, u32[]{:S(2)}) collective-permute-start(bf16[96,768]{1,0:T(8,128)(2,1)S(1)} %get-tuple-element.41.refs_0_), channel_id=1, source_target_pairs={{0,1},{1,2},{2,3},{3,4},{4,5},{5,6},{6,7},{7,0},{8,9},{9,10},{10,1... | collective-permute-start | bytes 442376 | tf_op jit(solution)/shard_map/ppermute | solution.py:34
  45.3 8.1 %collective-permute-start.2 = (bf16[96,768]{1,0:T(8,128)(2,1)S(1)}, bf16[96,768]{1,0:T(8,128)(2,1)S(1)}, u32[]{:S(2)}, u32[]{:S(2)}) collective-permute-start(bf16[96,768]{1,0:T(8,128)(2,1)S(1)} %get-tuple-element.41.refs_0_), channel_id=1, source_target_pairs={{0,7},{1,0},{2,1},{3,2},{4,3},{5,4},{6,5},{7,6},{8,15},{9,8},{10,9... | collective-permute-start | bytes 442376 | tf_op jit(solution)/shard_map/ppermute | solution.py:34
  53.4 6.0 %collective-permute-start.3 = (bf16[96,768]{1,0:T(8,128)(2,1)S(1)}, bf16[96,768]{1,0:T(8,128)(2,1)S(1)}, u32[]{:S(2)}, u32[]{:S(2)}) collective-permute-start(bf16[96,768]{1,0:T(8,128)(2,1)S(1)} %collective-permute-done.1.refs_1_), channel_id=1, source_target_pairs={{0,1},{1,2},{2,3},{3,4},{4,5},{5,6},{6,7},{7,0},{8,9},{9,10},{10,1... | collective-permute-start | bytes 442376 | tf_op jit(solution)/shard_map/ppermute | solution.py:34
  53.4 6.0 %collective-permute-start.4 = (bf16[96,768]{1,0:T(8,128)(2,1)S(1)}, bf16[96,768]{1,0:T(8,128)(2,1)S(1)}, u32[]{:S(2)}, u32[]{:S(2)}) collective-permute-start(bf16[96,768]{1,0:T(8,128)(2,1)S(1)} %collective-permute-done.2.refs_2_), channel_id=1, source_target_pairs={{0,7},{1,0},{2,1},{3,2},{4,3},{5,4},{6,5},{7,6},{8,15},{9,8},{10,9... | collective-permute-start | bytes 442376 | tf_op jit(solution)/shard_map/ppermute | solution.py:34
  59.3 5.6 %collective-permute-start.5 = (bf16[96,768]{1,0:T(8,128)(2,1)S(1)}, bf16[96,768]{1,0:T(8,128)(2,1)S(1)}, u32[]{:S(2)}, u32[]{:S(2)}) collective-permute-start(bf16[96,768]{1,0:T(8,128)(2,1)S(1)} %collective-permute-done.3.refs_3_), channel_id=1, source_target_pairs={{0,1},{1,2},{2,3},{3,4},{4,5},{5,6},{6,7},{7,0},{8,9},{9,10},{10,1... | collective-permute-start | bytes 442376 | tf_op jit(solution)/shard_map/ppermute | solution.py:34
  59.3 5.6 %collective-permute-start.6 = (bf16[96,768]{1,0:T(8,128)(2,1)S(1)}, bf16[96,768]{1,0:T(8,128)(2,1)S(1)}, u32[]{:S(2)}, u32[]{:S(2)}) collective-permute-start(bf16[96,768]{1,0:T(8,128)(2,1)S(1)} %collective-permute-done.4.refs_4_), channel_id=1, source_target_pairs={{0,7},{1,0},{2,1},{3,2},{4,3},{5,4},{6,5},{7,6},{8,15},{9,8},{10,9... | collective-permute-start | bytes 442376 | tf_op jit(solution)/shard_map/ppermute | solution.py:34
  64.9 4.8 %collective-permute-start.7 = (bf16[48,768]{1,0:T(8,128)(2,1)S(1)}, bf16[48,768]{1,0:T(8,128)(2,1)S(1)}, u32[]{:S(2)}, u32[]{:S(2)}) collective-permute-start(bf16[48,768]{1,0:T(8,128)(2,1)S(1)} %slice.8), channel_id=1, source_target_pairs={{0,1},{1,2},{2,3},{3,4},{4,5},{5,6},{6,7},{7,0},{8,9},{9,10},{10,1... | collective-permute-start | bytes 221192 | tf_op jit(solution)/shard_map/ppermute | solution.py:34
  65.0 4.8 %collective-permute-start.8 = (bf16[48,768]{1,0:T(8,128)(2,1)S(1)}, bf16[48,768]{1,0:T(8,128)(2,1)S(1)}, u32[]{:S(2)}, u32[]{:S(2)}) collective-permute-start(bf16[48,768]{1,0:T(8,128)(2,1)S(1)} %slice.9), channel_id=1, source_target_pairs={{0,7},{1,0},{2,1},{3,2},{4,3},{5,4},{6,5},{7,6},{8,15},{9,8},{10,9... | collective-permute-start | bytes 221192 | tf_op jit(solution)/shard_map/ppermute | solution.py:34
  71.6 17.0 %collective-permute-start.9 = (bf16[96,3072]{1,0:T(8,128)(2,1)S(1)}, bf16[96,3072]{1,0:T(8,128)(2,1)S(1)}, u32[]{:S(2)}, u32[]{:S(2)}) collective-permute-start(bf16[96,3072]{1,0:T(8,128)(2,1)S(1)} %get-tuple-element.42), channel_id=1, source_target_pairs={{0,8},{8,0},{1,9},{9,1},{2,10},{10,2},{3,11},{11,3},{4,12},{12,4},... | collective-permute-start | bytes 1769480 | tf_op jit(solution)/shard_map/ppermute | solution.py:38
  98.7 6.9 %collective-permute-start.11 = (bf16[112,1152]{1,0:T(8,128)(2,1)S(1)}, bf16[112,1152]{1,0:T(8,128)(2,1)S(1)}, u32[]{:S(2)}, u32[]{:S(2)}) collective-permute-start(bf16[112,1152]{1,0:T(8,128)(2,1)S(1)} %shard_map.81.refs_0_), channel_id=1, source_target_pairs={{0,16},{8,72},{16,32},{24,88},{32,48},{40,104},{48,0},{56,120},{64... | collective-permute-start | bytes 774152 | tf_op jit(solution)/shard_map/ppermute | solution.py:50
  98.8 8.7 %collective-permute-start.12 = (bf16[112,1152]{1,0:T(8,128)(2,1)S(1)}, bf16[112,1152]{1,0:T(8,128)(2,1)S(1)}, u32[]{:S(2)}, u32[]{:S(2)}) collective-permute-start(bf16[112,1152]{1,0:T(8,128)(2,1)S(1)} %shard_map.81.refs_0_), channel_id=1, source_target_pairs={{0,48},{8,200},{16,0},{24,216},{32,16},{40,232},{48,32},{56,248},{... | collective-permute-start | bytes 774152 | tf_op jit(solution)/shard_map/ppermute | solution.py:50
  101.5 7.0 %collective-permute-start.13 = (bf16[112,1152]{1,0:T(8,128)(2,1)S(1)}, bf16[112,1152]{1,0:T(8,128)(2,1)S(1)}, u32[]{:S(2)}, u32[]{:S(2)}) collective-permute-start(bf16[112,1152]{1,0:T(8,128)(2,1)S(1)} %shard_map.81.refs_0_), channel_id=1, source_target_pairs={{0,32},{8,136},{16,48},{24,152},{32,0},{40,168},{48,16},{56,184},{... | collective-permute-start | bytes 774152 | tf_op jit(solution)/shard_map/ppermute | solution.py:50
  108.5 14.6 %collective-permute-start.14 = (bf16[384,1152]{1,0:T(8,128)(2,1)S(1)}, bf16[384,1152]{1,0:T(8,128)(2,1)S(1)}, u32[]{:S(2)}, u32[]{:S(2)}) collective-permute-start(bf16[384,1152]{1,0:T(8,128)(2,1)S(1)} %get-tuple-element.57.refs_0_), channel_id=1, source_target_pairs={{0,64},{8,24},{16,80},{24,40},{32,96},{40,56},{48,112},{56,8},{64,... | collective-permute-start | bytes 2654216 | tf_op jit(solution)/shard_map/ppermute | solution.py:50
  108.6 14.6 %collective-permute-start.15 = (bf16[384,1152]{1,0:T(8,128)(2,1)S(1)}, bf16[384,1152]{1,0:T(8,128)(2,1)S(1)}, u32[]{:S(2)}, u32[]{:S(2)}) collective-permute-start(bf16[384,1152]{1,0:T(8,128)(2,1)S(1)} %get-tuple-element.57.refs_0_), channel_id=1, source_target_pairs={{0,192},{8,56},{16,208},{24,8},{32,224},{40,24},{48,240},{56,40},{... | collective-permute-start | bytes 2654216 | tf_op jit(solution)/shard_map/ppermute | solution.py:50
  111.3 4.9 %collective-permute-start.16 = (f32[8,128]{1,0:T(8,128)S(1)}, f32[8,128]{1,0:T(8,128)S(1)}, u32[]{:S(2)}, u32[]{:S(2)}) collective-permute-start(f32[8,128]{1,0:T(8,128)S(1)} %get-tuple-element.58), channel_id=1, source_target_pairs={{0,1},{1,2},{2,3},{3,4},{4,5},{5,6},{6,7},{7,0},{8,9},{9,10},{10,1... | collective-permute-start | bytes 12296 | tf_op jit(solution)/shard_map/ppermute | solution.py:34
  111.3 5.4 %collective-permute-start.17 = (f32[8,128]{1,0:T(8,128)S(1)}, f32[8,128]{1,0:T(8,128)S(1)}, u32[]{:S(2)}, u32[]{:S(2)}) collective-permute-start(f32[8,128]{1,0:T(8,128)S(1)} %get-tuple-element.58), channel_id=1, source_target_pairs={{0,2},{1,3},{2,4},{3,5},{4,6},{5,7},{6,0},{7,1},{8,10},{9,11},{10,... | collective-permute-start | bytes 12296 | tf_op jit(solution)/shard_map/ppermute | solution.py:34
  114.8 5.6 %collective-permute-start.18 = (f32[8,128]{1,0:T(8,128)S(1)}, f32[8,128]{1,0:T(8,128)S(1)}, u32[]{:S(2)}, u32[]{:S(2)}) collective-permute-start(f32[8,128]{1,0:T(8,128)S(1)} %get-tuple-element.58), channel_id=1, source_target_pairs={{0,3},{1,4},{2,5},{3,6},{4,7},{5,0},{6,1},{7,2},{8,11},{9,12},{10,... | collective-permute-start | bytes 12296 | tf_op jit(solution)/shard_map/ppermute | solution.py:34
  123.2 13.5 %collective-permute-start.20 = (bf16[384,1152]{1,0:T(8,128)(2,1)S(1)}, bf16[384,1152]{1,0:T(8,128)(2,1)S(1)}, u32[]{:S(2)}, u32[]{:S(2)}) collective-permute-start(bf16[384,1152]{1,0:T(8,128)(2,1)S(1)} %collective-permute-done.14.refs_1_), channel_id=1, source_target_pairs={{0,64},{8,24},{16,80},{24,40},{32,96},{40,56},{48,112},{56,8},{64,... | collective-permute-start | bytes 2654216 | tf_op jit(solution)/shard_map/ppermute | solution.py:50
  123.3 6.5 %collective-permute-start.21 = (f32[8,128]{1,0:T(8,128)S(1)}, f32[8,128]{1,0:T(8,128)S(1)}, u32[]{:S(2)}, u32[]{:S(2)}) collective-permute-start(f32[8,128]{1,0:T(8,128)S(1)} %add.21), channel_id=1, source_target_pairs={{0,4},{1,5},{2,6},{3,7},{4,0},{5,1},{6,2},{7,3},{8,12},{9,13},{10,... | collective-permute-start | bytes 12296 | tf_op jit(solution)/shard_map/ppermute | solution.py:34
  129.7 6.7 %collective-permute-start.22 = (f32[8,128]{1,0:T(8,128)S(1)}, f32[8,128]{1,0:T(8,128)S(1)}, u32[]{:S(2)}, u32[]{:S(2)}) collective-permute-start(f32[8,128]{1,0:T(8,128)S(1)} %add.22), channel_id=1, source_target_pairs={{0,128},{8,40},{16,144},{24,56},{32,160},{40,8},{48,176},{56,24},{... | collective-permute-start | bytes 12296 | tf_op jit(solution)/shard_map/ppermute | solution.py:50
  137.1 7.4 %collective-permute-start.23 = (bf16[3,192,384]{2,1,0:T(8,128)(2,1)S(1)}, bf16[3,192,384]{2,1,0:T(8,128)(2,1)S(1)}, u32[]{:S(2)}, u32[]{:S(2)}) collective-permute-start(bf16[3,192,384]{2,1,0:T(8,128)(2,1)S(1)} %shard_map.85), channel_id=1, source_target_pairs={{0,8},{8,0},{1,9},{9,1},{2,10},{10,2},{3,11},{11,3},{4,12},{12,4},... | collective-permute-start | bytes 1327112 | tf_op jit(solution)/shard_map/ppermute | solution.py:38
  (5 other events, 8.5 us)
Sparse Core Ops, SparseCore 0:
  10.4 75.9 all-gather.6
  88.8 35.6 all-gather.4
